TPU v7x, 512 devices: a whole 4x8x8 slice. The times are simulated.
512 devices in a mesh: prow: 32 (over z, x), pcol: 16 (over y, core).
Axes of the slice: x: 4, y: 8, z: 8, core: 2. Of those that a mesh axis runs over, the one named last changes fastest.
Arguments:
- matrix: float32 [2, 8192, 4, 4096], P(None, 'prow', None, 'pcol'), may hold values from -40 to 150, as said below
- block_mask: int32 [64, 64], replicated, may hold values from 0 to 1, as said below
- first_panel: int32 [1], replicated, may hold values from 0 to 31
Outputs:
- factored: float32 [2, 8192, 4, 4096], P(None, 'prow', None, 'pcol')
Inputs may be any that keep to these rules, and one draw needn't show every extreme that they name: `block_mask`: symmetric, with ones on the diagonal and on the blocks right beside it. `matrix`: entries off the diagonal lie between -40 and 40, diagonal entries between 60 and 150; the symmetric part of the two diagonal blocks of rows and columns k and k + 1 together is positive definite for every k.
All inputs are finite; a program needn't handle non-finite values.
Results may differ from a plain program's by a relative error of at most 0.0003.
Values sent between devices are 32-bit elements; how exact they have to be, the bound alone decides.
A program may use at most 64 MiB of HBM per device.

v0:
```python
import jax
import jax.numpy as jnp
from jax import lax
from jax.sharding import PartitionSpec as P


def broadcast(block, axis, holder):
    block = jnp.where(lax.axis_index(axis) == holder, block, jnp.zeros_like(block))
    return lax.psum(block, axis)


def solve_blocks(diag_lower, raw_panel):
    block_count, block_width, _ = raw_panel.shape
    flattened = raw_panel.reshape(block_count * block_width, block_width).T
    solved = jax.scipy.linalg.solve_triangular(diag_lower, flattened, lower=True)
    return solved.T.reshape(block_count, block_width, block_width)


def shifted_factor(diag_input):
    identity = jnp.eye(diag_input.shape[0], dtype=jnp.float32)
    return jnp.linalg.cholesky(diag_input + identity)


def column_panel(row_panel, my_col):
    stride = lax.axis_size("pcol")
    group_size = lax.axis_size("prow") // stride
    received = []
    for source in range(group_size):
        received.append(broadcast(row_panel, "prow", my_col + source * stride))
    stacked = jnp.stack(received, axis=1)
    return stacked.reshape(-1, row_panel.shape[1], row_panel.shape[2])


def factor_panel(column, panel_index, row_ids, my_col):
    n_rows = lax.axis_size("prow")
    n_cols = lax.axis_size("pcol")
    owner_row = panel_index % n_rows
    owner_col = panel_index % n_cols
    candidate = lax.dynamic_index_in_dim(column, panel_index // n_rows, 0, keepdims=False)
    below_panel = row_ids > panel_index
    raw_panel = jnp.where(below_panel[:, None, None], column, jnp.float32(0.0))
    diag_input = broadcast(candidate, "prow", owner_row)
    diag_lower = shifted_factor(diag_input)
    row_panel = broadcast(solve_blocks(diag_lower, raw_panel), "pcol", owner_col)
    col_panel = column_panel(row_panel, my_col)
    return (row_panel, col_panel, diag_lower)


def write_column(current, panel_index, row_panel, diag_lower, row_ids, my_col):
    n_cols = lax.axis_size("pcol")
    slot_col = panel_index // n_cols
    column = lax.dynamic_index_in_dim(current, slot_col, 2, keepdims=False)
    renewed = jnp.where(
        (row_ids > panel_index)[:, None, None],
        row_panel,
        jnp.where((row_ids == panel_index)[:, None, None], diag_lower[None], column),
    )
    renewed = jnp.where(my_col == panel_index % n_cols, renewed, column)
    return lax.dynamic_update_index_in_dim(current, renewed, slot_col, 2)


def trailing(current, panel_index, row_panel, col_panel, row_ids, col_ids):
    update = jnp.einsum("sab,tcb->satc", row_panel, col_panel, precision=lax.Precision.HIGHEST)
    active = (
        (row_ids[:, None] > panel_index)
        & (col_ids[None, :] > panel_index)
        & (row_ids[:, None] >= col_ids[None, :])
    )
    return jnp.where(active[:, None, :, None], current - update, current)


def local(matrix, block_mask, first_panel):
    n_rows = lax.axis_size("prow")
    n_cols = lax.axis_size("pcol")
    my_row = lax.axis_index("prow")
    my_col = lax.axis_index("pcol")
    row_ids = jnp.arange(matrix.shape[0], dtype=jnp.int32) * n_rows + my_row
    col_ids = jnp.arange(matrix.shape[2], dtype=jnp.int32) * n_cols + my_col
    local_mask = block_mask[row_ids[:, None], col_ids[None, :]]
    kept_blocks = (local_mask == 1) & (row_ids[:, None] >= col_ids[None, :])
    current = jnp.where(kept_blocks[:, None, :, None], matrix, jnp.float32(0.0))
    first_index = first_panel[0]
    second = first_index + 1
    column_first = lax.dynamic_index_in_dim(current, first_index // n_cols, 2, keepdims=False)
    rows_first, cols_first, diag_first = factor_panel(column_first, first_index, row_ids, my_col)
    current = write_column(current, first_index, rows_first, diag_first, row_ids, my_col)
    current = trailing(current, first_index, rows_first, cols_first, row_ids, col_ids)
    column_next = lax.dynamic_index_in_dim(current, second // n_cols, 2, keepdims=False)
    rows_next, cols_next, diag_next = factor_panel(column_next, second, row_ids, my_col)
    current = write_column(current, second, rows_next, diag_next, row_ids, my_col)
    return trailing(current, second, rows_next, cols_next, row_ids, col_ids)


def solution(mesh):
    in_specs = (P(None, "prow", None, "pcol"), P(), P())
    out_specs = P(None, "prow", None, "pcol")
    return jax.shard_map(local, mesh=mesh, in_specs=in_specs, out_specs=out_specs, check_vma=False)
```

profile of v0, /device:TPU:56, one launch (start us, length us, event | category | flops | bytes accessed | tf_op | source)
XLA Modules:
  0.0 1071.0 jit_solution(15569107883818967229)
XLA Ops:
  7.2 2.9 copy.15
  16.2 157.2 %all-reduce.10.cloned.1.call-done = f32[256,256]{0,1:T(8,128)} async-done(((f32[256,256]{0,1:T(8,128)}), f32[256,256]{0,1:T(8,128)}) %all-reduce.10.cloned.1.call-update) | async-done | bytes 262160 | tf_op jit(solution)/shard_map/psum | solution.py:9
  177.9 11.7 %cholesky.130 = f32[128,128]{1,0:T(8,128)S(1)} custom-call(f32[128,128]{1,0:T(8,128)S(1)} %cholesky.194), custom_call_target="Cholesky" | custom-call | tf_op jit(solution)/shard_map/jit(cholesky)/cholesky | solution.py:21
  190.3 10.6 custom-call.15
  203.7 12.5 %cholesky.147 = f32[128,128]{1,0:T(8,128)S(1)} custom-call(f32[128,128]{1,0:T(8,128)} %convolution_subtract_fusion.3), custom_call_target="Cholesky" | custom-call | tf_op jit(solution)/shard_map/jit(cholesky)/cholesky | solution.py:21
  221.4 5.4 while.4
  226.8 21.1 %custom-call.16 = f32[2,128,128]{1,2,0:T(8,128)} custom-call(f32[2,128,128]{2,1,0:T(8,128)} %get-tuple-element.21), custom_call_target="InvertDiagBlocksLowerTriangular" | custom-call | tf_op jit(solution)/shard_map/jit(_solve_triangular)/triangular_solve | solution.py:15
  254.2 109.7 %all-reduce.12.cloned.1.call-done = f32[2,256,256]{1,2,0:T(8,128)} async-done(((f32[2,256,256]{1,2,0:T(8,128)}), f32[2,256,256]{1,2,0:T(8,128)}) %all-reduce.12.cloned.1.call-update) | async-done | bytes 524304 | tf_op jit(solution)/shard_map/psum | solution.py:9
  368.3 163.4 %all-reduce.20.cloned.1.call-done = (f32[2,1,256,256]{2,3,0,1:T(8,128)}, f32[2,1,256,256]{2,3,0,1:T(8,128)}) async-done(((f32[2,1,256,256]{2,3,0,1:T(8,128)}, f32[2,1,256,256]{2,3,0,1:T(8,128)}), (f32[2,1,256,256]{2,3,0,1:T(8,128)}, f32[2,1,256,256]{2,3,0,1:T(8,128)})) %all-reduce.20.cloned.1.call-update) | async-done | bytes 1048592 | tf_op jit(solution)/shard_map/psum | solution.py:9
  531.8 2.3 pad_maximum_fusion
  534.0 2.6 copy.22
  536.6 3.8 subtract_select_fusion.1
  543.7 150.1 %all-reduce.14.cloned.1.call-done = f32[256,256]{0,1:T(8,128)} async-done(((f32[256,256]{0,1:T(8,128)}), f32[256,256]{0,1:T(8,128)}) %all-reduce.14.cloned.1.call-update) | async-done | bytes 262160 | tf_op jit(solution)/shard_map/psum | solution.py:9
  698.2 11.7 %cholesky.164 = f32[128,128]{1,0:T(8,128)S(1)} custom-call(f32[128,128]{1,0:T(8,128)S(1)} %cholesky.197), custom_call_target="Cholesky" | custom-call | tf_op jit(solution)/shard_map/jit(cholesky)/cholesky | solution.py:21
  710.6 10.6 custom-call.17
  724.0 12.5 %cholesky.181 = f32[128,128]{1,0:T(8,128)S(1)} custom-call(f32[128,128]{1,0:T(8,128)} %convolution_subtract_fusion.2), custom_call_target="Cholesky" | custom-call | tf_op jit(solution)/shard_map/jit(cholesky)/cholesky | solution.py:21
  741.6 5.5 while.5
  747.0 21.1 %custom-call.18 = f32[2,128,128]{1,2,0:T(8,128)} custom-call(f32[2,128,128]{2,1,0:T(8,128)} %get-tuple-element.22), custom_call_target="InvertDiagBlocksLowerTriangular" | custom-call | tf_op jit(solution)/shard_map/jit(_solve_triangular)/triangular_solve | solution.py:15
  774.5 109.8 %all-reduce.16.cloned.1.call-done = f32[2,256,256]{1,2,0:T(8,128)} async-done(((f32[2,256,256]{1,2,0:T(8,128)}), f32[2,256,256]{1,2,0:T(8,128)}) %all-reduce.16.cloned.1.call-update) | async-done | bytes 524304 | tf_op jit(solution)/shard_map/psum | solution.py:9
  888.4 163.1 %all-reduce.18.cloned.1.call-done = (f32[2,1,256,256]{2,3,0,1:T(8,128)}, f32[2,1,256,256]{2,3,0,1:T(8,128)}) async-done(((f32[2,1,256,256]{2,3,0,1:T(8,128)}, f32[2,1,256,256]{2,3,0,1:T(8,128)}), (f32[2,1,256,256]{2,3,0,1:T(8,128)}, f32[2,1,256,256]{2,3,0,1:T(8,128)})) %all-reduce.18.cloned.1.call-update) | async-done | bytes 1048592 | tf_op jit(solution)/shard_map/psum | solution.py:9
  1051.5 2.3 pad_maximum_fusion.1
  1053.8 2.5 copy.30
  1056.3 4.5 subtract_select_fusion
  1060.8 2.9 copy.33
  (115 shorter events, 63.9 us)
Async XLA Ops:
  6.5 3.8 copy-start
  6.5 166.9 %all-reduce.10.cloned.1.call-start = ((), (), s32[]{:S(2)}) async-start(), calls=%async_computation | async-start | bytes 524288 | tf_op jit(solution)/shard_map/psum | solution.py:9
  13.8 350.1 %all-reduce.12.cloned.1.call-start = ((), (), s32[]{:S(2)}) async-start(), calls=%async_computation.1 | async-start | bytes 1048576 | tf_op jit(solution)/shard_map/psum | solution.py:9
  177.2 0.7 copy-start.8
  217.0 1.9 copy-start.4
  252.0 114.3 %copy-start.6 = (f32[256,256]{1,0:T(8,128)S(1)}, f32[256,256]{1,0:T(8,128)}, u32[]{:S(2)}) copy-start(f32[256,256]{1,0:T(8,128)} %get-tuple-element.46) | copy-start | bytes 786436
  254.1 277.6 %all-reduce.20.cloned.1.call-start = ((), (), s32[]{:S(2)}) async-start(), calls=%async_computation.5 | async-start | bytes 2097152 | tf_op jit(solution)/shard_map/psum | solution.py:9
  363.9 3.3 copy-start.2
  366.1 327.6 %all-reduce.14.cloned.1.call-start = ((), (), s32[]{:S(2)}) async-start(), calls=%async_computation.2 | async-start | bytes 524288 | tf_op jit(solution)/shard_map/psum | solution.py:9
  368.3 168.3 %copy-start.1 = (f32[2,256,4,256]{1,3,2,0:T(8,128)}, f32[2,256,4,256]{1,3,2,0:T(8,128)S(1)}, u32[]{:S(2)}) copy-start(f32[2,256,4,256]{1,3,2,0:T(8,128)S(1)} %bitcast_dynamic-update-slice_fusion.2) | copy-start | bytes 6291460
  541.2 343.1 %all-reduce.16.cloned.1.call-start = ((), (), s32[]{:S(2)}) async-start(), calls=%async_computation.3 | async-start | bytes 1048576 | tf_op jit(solution)/shard_map/psum | solution.py:9
  697.5 0.7 copy-start.9
  737.3 1.9 copy-start.5
  772.3 114.1 %copy-start.7 = (f32[256,256]{1,0:T(8,128)S(1)}, f32[256,256]{1,0:T(8,128)}, u32[]{:S(2)}) copy-start(f32[256,256]{1,0:T(8,128)} %get-tuple-element.44) | copy-start | bytes 786436
  774.4 277.1 %all-reduce.18.cloned.1.call-start = ((), (), s32[]{:S(2)}) async-start(), calls=%async_computation.4 | async-start | bytes 2097152 | tf_op jit(solution)/shard_map/psum | solution.py:9
  884.2 3.0 copy-start.3
Sparse Core Ops, SparseCore 0:
  13.9 159.4 all-reduce.9
  254.3 109.6 all-reduce.11
  367.9 163.7 all-reduce.19
  541.3 152.4 all-reduce.13
  774.5 109.6 all-reduce.15
  887.7 163.8 all-reduce.17
where the time goes:
time: 1080 us; the launch traced here: 1070 us
  waiting for transfers between devices  854 us (79%)
  other arithmetic  142 us (13%)
  local copies, waits for them, and re-layouts  37.2 us (3%)
  matrix products  20 us (2%)
  between operations  17.5 us (2%)
    psum x6, waiting for transfers between devices, broadcast(): return lax.psum(block, axis)  853 us
    another operation x14, other arithmetic, shifted_factor(): return jnp.linalg.cholesky(diag_input + identity)  73.8 us
    another operation x5, other arithmetic, solve_blocks(): jax.scipy.linalg.solve_triangular(diag_lower, flattened, lower=True)  45.6 us
  transfers between devices with their start and end apart: 6, of which 6 were waited for; matrix products, arithmetic and copies ran while one was open for 1% of the time, Pallas kernels for 0%

commit v1 on v0

v1 whole, which is shorter than its diff:
```python
import functools
import jax
import jax.numpy as jnp
from jax import lax
from jax.experimental import pallas as pl
from jax.experimental.pallas import tpu as pltpu
from jax.sharding import PartitionSpec as P

MESH = pl.DeviceIdType.MESH
HI = lax.Precision.HIGHEST
F32 = jnp.float32
B = 256
NB = 16


def piece_row(c):
    return NB * ((c % 2) * 8 + ((c // 2) % 2) * 4 + c // 4)


def tdot(a, b):
    return lax.dot_general(a, b, (((0,), (0,)), ((), ())), precision=HI, preferred_element_type=F32)


def ndot(a, b):
    return lax.dot_general(a, b, (((1,), (1,)), ((), ())), precision=HI, preferred_element_type=F32)


def inverse_factor(m, w, hook):
    rows = lax.broadcasted_iota(jnp.int32, (NB, 128), 0)
    lane = lax.broadcasted_iota(jnp.int32, (NB, B), 1)
    sub = lax.broadcasted_iota(jnp.int32, (NB, B), 0)
    nxt = m[0:NB, :]
    for p in range(B // NB):
        p0, q = p * NB, p * NB + NB
        inside = (lane >= p0) & (lane < q)
        t = [jnp.broadcast_to(nxt[:, p0 + c : p0 + c + 1], (NB, 128)) for c in range(NB)]
        x = jnp.where(inside, jnp.where(lane - p0 == sub, 1.0, 0.0), nxt)
        x0, x1 = x[:, :128], x[:, 128:]
        s = jnp.ones((NB, 128), F32)
        for j in range(NB):
            d = jnp.broadcast_to(t[j][j : j + 1, :], (NB, 128))
            s = jnp.where(rows == j, lax.rsqrt(d), s)
            mm = jnp.where(rows > j, t[j], 0.0) * (1.0 / d)
            for c in range(j + 1, NB):
                t[c] = t[c] - mm * jnp.broadcast_to(t[c][j : j + 1, :], (NB, 128))
            x0 = x0 - mm * jnp.broadcast_to(x0[j : j + 1, :], (NB, 128))
            x1 = x1 - mm * jnp.broadcast_to(x1[j : j + 1, :], (NB, 128))
        rr = jnp.concatenate([x0 * s, x1 * s], axis=1)
        w[p0:q, :] = jnp.where(lane < q, rr, 0.0)
        if q < B:
            nxt = jnp.where(inside, 0.0, m[q : q + NB, :]) - tdot(rr[:, q : q + NB], rr)
        if q + NB < B:
            wide = lax.broadcasted_iota(jnp.int32, (B - q - NB, B), 1)
            rest = m[q + NB :, :]
            m[q + NB :, :] = jnp.where((wide >= p0) & (wide < q), 0.0, rest) - tdot(rr[:, q + NB :], rr)
        hook(p)


def gather_kernel(
    k_ref, x_ref, e_ref, rows_ref, cols_ref, fac_ref,
    rsb, hb, own, low, g12, work,
    rs_s, rs_r, g_s, g_r, cs_s, cs_r, ag_s, ag_r, sib_s, sib_r, zc_s, zc_r, xc_s, xc_r, xf_s, xf_r,
    w_s, w_r, loc,
):
    r, c = lax.axis_index("prow"), lax.axis_index("pcol")
    z, x, y, h = r // 4, r % 4, c // 2, c % 2
    k = k_ref[0]
    cand = (r % 16) == c
    u, rest = r // 16, r % 16
    to_col = (c + 16 * u, rest)
    below = (r + 31) % 32
    home = (below, below % 16)
    is_sub = ((r + 31) % 16) == c

    def at(dz=0, dx=0, dy=0, core=None):
        zz, xx, yy = (z + dz) % 8, (x + dx) % 4, (y + dy) % 8
        return (zz * 4 + xx, yy * 2 + (h if core is None else core))

    def relay_y(zz, m):
        return (2 * zz + m // 2 + 3 + zz // 4) % 8

    is_holder = (x < 3) & (y == relay_y(z, x))

    def remote(src, dst, ss, rs, to):
        return pltpu.make_async_remote_copy(
            src_ref=src, dst_ref=dst, send_sem=ss, recv_sem=rs, device_id=to, device_id_type=MESH
        )

    def drain(ref, sem):
        pltpu.make_async_copy(ref, ref, sem).wait()

    bar = pltpu.get_barrier_semaphore()

    def greet(to):
        pl.semaphore_signal(bar, inc=1, device_id=to, device_id_type=MESH)

    for j in range(1, 16):
        greet((r, (c + j) % 16))
    for j in range(1, 8):
        greet(at(dz=j))
    for j in range(1, 4):
        greet(at(dx=j))

    @pl.when(jnp.logical_not(cand))
    def _():
        greet((c + 16 * u, rest))

    @pl.when(cand)
    def _():
        up = (r + 1) % 32
        greet((up, up % 16))
        greet((up, r % 16))

    @pl.when(is_holder)
    def _():
        def one(i, carry):
            greet((i, i % 16))
            return carry

        lax.fori_loop(0, 32, one, 0)

    arrivals = 15 + 7 + 3 + jnp.where(cand, 49, 1) + jnp.where(is_sub, 1, 0)
    mine = pl.ds(pl.multiple_of(piece_row(c), NB), NB)

    def first_sends():
        pl.semaphore_wait(bar, arrivals)

        @pl.when(is_sub)
        def _():
            remote(e_ref.at[1], g12.at[0], g_s.at[0], g_r.at[0], home).start()

        @pl.when(cand)
        def _():
            remote(e_ref.at[2], g12.at[1], g_s.at[1], g_r.at[1], home).start()

        for j in range(1, 16):
            to = (c + j) % 16
            row = pl.multiple_of(piece_row(to), NB)
            remote(x_ref.at[:, pl.ds(row, NB), :], rsb.at[c], rs_s, rs_r, (r, to)).start()

    rsb[c] = x_ref[:, mine, :]
    theirs = pl.ds(pl.multiple_of(piece_row(rest), NB), NB)

    def pick_rows():
        drain(rsb.at[pl.ds(0, 15)], rs_r)
        rows_ref[0, :, mine, :] = rsb[k % 16]
        rows_ref[1, :, mine, :] = rsb[(k + 1) % 16]
        piece = rows_ref.at[:, :, mine, :]

        @pl.when(jnp.logical_not(cand))
        def _():
            remote(piece, cols_ref.at[u, :, :, mine, :], cs_s, cs_r, to_col).start()

        @pl.when(cand)
        def _():
            cols_ref[u, :, :, mine, :] = rows_ref[:, :, mine, :]

        for j in range(1, 8):
            remote(piece, piece, ag_s, ag_r, at(dy=j)).start()

    def send_z():
        piece = cols_ref.at[u, :, :, theirs, :]

        @pl.when(jnp.logical_not(cand))
        def _():
            drain(piece, cs_r)

        for j in range(1, 8):
            remote(piece, piece, zc_s, zc_r, at(dz=j)).start()

    def send_sibling():
        drain(rows_ref.at[:, :, pl.ds(0, 7 * NB), :], ag_r)
        half = rows_ref.at[:, :, pl.ds(pl.multiple_of(128 * h, 128), 128), :]
        remote(half, half, sib_s, sib_r, at(core=1 - h)).start()

    def quarter(xx):
        return pl.ds(pl.multiple_of(NB * (8 * (xx % 2) + 4 * ((xx // 2) % 2)), 64), 64)

    def send_x():
        drain(cols_ref.at[0, :, :, pl.ds(0, 7 * NB), :], zc_r)
        part = cols_ref.at[:, :, :, quarter(x), :]
        remote(part, part, xc_s.at[0], xc_r.at[0], at(dx=1)).start()
        remote(part, part, xc_s.at[1], xc_r.at[1], at(dx=3)).start()

    def forward_x():
        for way, dx in ((0, 1), (1, 3)):
            part = cols_ref.at[:, :, :, quarter(x + 4 - dx), :]
            drain(part, xc_r.at[way])
            half = cols_ref.at[way, :, :, quarter(x + 4 - dx), :]
            remote(half, half, xf_s.at[way], xf_r.at[way], at(dx=dx)).start()

    def scatter_factor(m, pieces=range(16)):
        for p in pieces:
            zz, core = p % 8, p // 8
            to = (zz * 4 + m, relay_y(zz, m) * 2 + core)
            remote(low.at[m, pl.ds(p * NB, NB), :], hb.at[r], w_s.at[m, 0], w_r.at[m, 0], to).start()

    slab = pl.ds(pl.multiple_of(128 * h + NB * z, NB), NB)

    def relay_factor(m, stage):
        piece = fac_ref.at[m, slab, :]
        if stage == 0:

            @pl.when(is_holder & (x == m))
            def _():
                drain(hb, w_r.at[m, 0])
                fac_ref[m, slab, :] = hb[k]
                for j in range(1, 4):
                    remote(piece, piece, w_s.at[m, 1], w_r.at[m, 1], at(dx=j)).start()

        elif stage == 1:

            @pl.when(y == relay_y(z, m))
            def _():
                @pl.when(x != m)
                def _():
                    drain(piece, w_r.at[m, 1])

                for j in range(1, 8):
                    remote(piece, piece, w_s.at[m, 2], w_r.at[m, 2], at(dy=j)).start()

        elif stage == 2:

            @pl.when(y != relay_y(z, m))
            def _():
                drain(piece, w_r.at[m, 2])

            for j in range(1, 8):
                remote(piece, piece, w_s.at[m, 3], w_r.at[m, 3], at(dz=j)).start()
        elif stage == 3:
            drain(fac_ref.at[m, pl.ds(0, 7 * NB), :], w_r.at[m, 3])
            half = fac_ref.at[m, pl.ds(pl.multiple_of(128 * h, 128), 128), :]
            remote(half, half, w_s.at[m, 4], w_r.at[m, 4], at(core=1 - h)).start()

    eye = jnp.where(
        lax.broadcasted_iota(jnp.int32, (B, B), 0) == lax.broadcasted_iota(jnp.int32, (B, B), 1), 1.0, 0.0
    ).astype(F32)

    @pl.when(cand)
    def _():
        a = e_ref[0]
        work[...] = (a + a.T) * 0.5 + eye

        def first_hook(p):
            if p == 4:
                first_sends()
                scatter_factor(0, range(5))
            elif p > 4:
                scatter_factor(0, [p])

        inverse_factor(work, low.at[0], first_hook)
        drain(g12.at[0], g_r.at[0])
        drain(g12.at[1], g_r.at[1])
        l21 = ndot(g12[0], low[0])
        low[1] = l21
        scatter_factor(1)
        d = g12[1]
        work[...] = (d + d.T) * 0.5 + eye - ndot(l21, l21)

        def second_hook(p):
            scatter_factor(2, [p])
            if p == 2:
                pick_rows()
            if p == 7:
                send_z()
            if p == 10:
                relay_factor(0, 1)
            if p == 12:
                relay_factor(1, 1)
            if p == 15:
                relay_factor(0, 2)

        inverse_factor(work, low.at[2], second_hook)
        relay_factor(1, 2)
        send_sibling()

    @pl.when(jnp.logical_not(cand))
    def _():
        first_sends()
        pick_rows()
        send_z()
        for stage in range(3):
            for m in range(2):
                relay_factor(m, stage)
        send_sibling()

    relay_factor(0, 3)
    relay_factor(1, 3)
    relay_factor(2, 0)
    send_x()
    relay_factor(2, 1)
    relay_factor(2, 2)
    relay_factor(2, 3)
    forward_x()

    for m in range(3):
        drain(fac_ref.at[m, pl.ds(0, 128), :], w_r.at[m, 4])
    drain(rows_ref.at[:, :, pl.ds(0, 128), :], sib_r)
    for way, dx in ((0, 1), (1, 3)):
        drain(cols_ref.at[way, :, :, quarter(x + 2), :], xf_r.at[way])

    @pl.when(is_sub)
    def _():
        drain(e_ref.at[1], g_s.at[0])

    @pl.when(cand)
    def _():
        drain(e_ref.at[2], g_s.at[1])
        for m in range(3):
            drain(low.at[m], w_s.at[m, 0])

    drain(rsb.at[pl.ds(0, 15)], rs_s)

    @pl.when(jnp.logical_not(cand))
    def _():
        drain(rows_ref.at[:, :, mine, :], cs_s)

    drain(rows_ref.at[:, :, pl.ds(0, 7 * NB), :], ag_s)
    drain(rows_ref.at[:, :, pl.ds(0, 128), :], sib_s)
    drain(cols_ref.at[0, :, :, pl.ds(0, 7 * NB), :], zc_s)
    for way in range(2):
        drain(cols_ref.at[:, :, :, quarter(x), :], xc_s.at[way])
        drain(cols_ref.at[way, :, :, quarter(x), :], xf_s.at[way])
    for m in range(3):

        @pl.when(is_holder & (x == m))
        def _():
            drain(fac_ref.at[m, pl.ds(0, 3 * NB), :], w_s.at[m, 1])

        @pl.when(y == relay_y(z, m))
        def _():
            drain(fac_ref.at[m, pl.ds(0, 7 * NB), :], w_s.at[m, 2])

        drain(fac_ref.at[m, pl.ds(0, 7 * NB), :], w_s.at[m, 3])
        drain(fac_ref.at[m, pl.ds(0, 128), :], w_s.at[m, 4])


def split(a):
    hi = a.astype(jnp.bfloat16)
    return hi, (a - hi.astype(F32)).astype(jnp.bfloat16)


def dot3(a, b):
    dims = (((1,), (1,)), ((), ()))
    one = lambda u, v: lax.dot_general(u, v, dims, preferred_element_type=F32)
    return one(a[0], b[0]) + (one(a[0], b[1]) + one(a[1], b[0]))


def update_kernel(k_ref, mask_ref, m_ref, rows_ref, cols_ref, fac_ref, out_ref, l1h, l1l, l2h, l2l):
    r, c = lax.axis_index("prow"), lax.axis_index("pcol")
    k = k_ref[0]
    n = k + 1
    w1, l21, w2 = split(fac_ref[0]), split(fac_ref[1]), split(fac_ref[2])

    ids = [r, r + 32, c, c + 32, c + 16, c + 48]
    for v, i in enumerate(ids):
        if v < 2:
            a1, a2 = rows_ref[0, v], rows_ref[1, v]
        else:
            a1, a2 = cols_ref[v // 2 - 1, 0, v % 2], cols_ref[v // 2 - 1, 1, v % 2]
        a1 = jnp.where((mask_ref[i, k] == 1) & (i > k), a1, 0.0)
        a2 = jnp.where((mask_ref[i, n] == 1) & (i > n), a2, 0.0)
        p1 = split(dot3(split(a1), w1))
        a2 = jnp.where(i > n, a2 - dot3(p1, l21), 0.0)
        p2 = split(dot3(split(a2), w2))
        l1h[v], l1l[v] = p1
        l2h[v], l2l[v] = p2

    col_slot = [2, 4, 3, 5]
    for s in range(2):
        i = r + 32 * s
        for t in range(4):
            j = c + 16 * t
            v = col_slot[t]
            lower = i >= j
            if s == 0 and t >= 2:
                out_ref[s, :, t, :] = jnp.zeros((B, B), F32)
                continue
            base = jnp.where((mask_ref[i, j] == 1) & lower, m_ref[s, :, t, :], 0.0)
            upd = dot3((l1h[s], l1l[s]), (l1h[v], l1l[v])) + dot3((l2h[s], l2l[s]), (l2h[v], l2l[v]))
            out_ref[s, :, t, :] = base - jnp.where(lower, upd, 0.0)

    eye = jnp.where(
        lax.broadcasted_iota(jnp.int32, (B, B), 0) == lax.broadcasted_iota(jnp.int32, (B, B), 1), 1.0, 0.0
    ).astype(F32)
    for s in range(2):
        i = r + 32 * s
        for t in range(3):
            j = c + 16 * t

            @pl.when((j == k) & (i > k))
            def _():
                out_ref[s, :, t, :] = l1h[s].astype(F32) + l1l[s].astype(F32)

            @pl.when((j == n) & (i > n))
            def _():
                out_ref[s, :, t, :] = l2h[s].astype(F32) + l2l[s].astype(F32)

            @pl.when((j == k) & (i == k))
            def _():
                a = m_ref[s, :, t, :]
                f = ndot((a + a.T) * 0.5 + eye, fac_ref[0])
                low = lax.broadcasted_iota(jnp.int32, (B, B), 0) >= lax.broadcasted_iota(jnp.int32, (B, B), 1)
                out_ref[s, :, t, :] = jnp.where(low, f, 0.0)

            @pl.when((j == n) & (i == n))
            def _():
                a = m_ref[s, :, t, :]
                g = fac_ref[1]
                f = ndot((a + a.T) * 0.5 + eye - ndot(g, g), fac_ref[2])
                low = lax.broadcasted_iota(jnp.int32, (B, B), 0) >= lax.broadcasted_iota(jnp.int32, (B, B), 1)
                out_ref[s, :, t, :] = jnp.where(low, f, 0.0)


def vmem():
    return pl.BlockSpec(memory_space=pltpu.VMEM)


def smem():
    return pl.BlockSpec(memory_space=pltpu.SMEM)


def local(matrix, block_mask, first_panel):
    r, c = lax.axis_index("prow"), lax.axis_index("pcol")
    k = first_panel[0]
    t = jnp.where(c == k % 16, k // 16, (k + 1) // 16)
    x = lax.dynamic_index_in_dim(matrix, t, 2, keepdims=False)

    def block(s, t):
        return lax.dynamic_slice(matrix, (s, 0, t, 0), (1, B, 1, B)).reshape(B, B)

    top = (r == 0).astype(jnp.int32)
    e = jnp.stack([block(0, r // 16), block(top, (r - 1 + 32 * top) // 16), block(top, r // 16 + 2 * top)])
    dma = pltpu.SemaphoreType.DMA
    rows, cols, fac = pl.pallas_call(
        gather_kernel,
        out_shape=(
            jax.ShapeDtypeStruct((2, 2, B, B), F32),
            jax.ShapeDtypeStruct((2, 2, 2, B, B), F32),
            jax.ShapeDtypeStruct((3, B, B), F32),
        ),
        in_specs=[smem(), vmem(), vmem()],
        out_specs=(vmem(), vmem(), vmem()),
        scratch_shapes=[
            pltpu.VMEM((16, 2, NB, B), F32),
            pltpu.VMEM((32, NB, B), F32),
            pltpu.VMEM((8, 128), F32),
            pltpu.VMEM((3, B, B), F32),
            pltpu.VMEM((2, B, B), F32),
            pltpu.VMEM((B, B), F32),
            dma, dma, dma((2,)), dma((2,)), dma, dma, dma, dma, dma, dma, dma, dma,
            dma((2,)), dma((2,)), dma((2,)), dma((2,)), dma((3, 5)), dma((3, 5)), dma,
        ],
        compiler_params=pltpu.CompilerParams(collective_id=0, has_side_effects=True, vmem_limit_bytes=40 << 20),
        cost_estimate=pl.CostEstimate(flops=10**9, bytes_accessed=10**7, transcendentals=0),
        name="gather_factor",
    )(first_panel, x, e)
    return pl.pallas_call(
        update_kernel,
        out_shape=jax.ShapeDtypeStruct(matrix.shape, F32),
        in_specs=[smem(), smem(), vmem(), vmem(), vmem(), vmem()],
        out_specs=vmem(),
        scratch_shapes=[pltpu.VMEM((6, B, B), jnp.bfloat16)] * 4,
        compiler_params=pltpu.CompilerParams(vmem_limit_bytes=48 << 20),
        cost_estimate=pl.CostEstimate(flops=4 * 10**9, bytes_accessed=10**7, transcendentals=0),
        name="update",
    )(first_panel, block_mask, matrix, rows, cols, fac)


def solution(mesh):
    spec = P(None, "prow", None, "pcol")
    return jax.shard_map(local, mesh=mesh, in_specs=(spec, P(), P()), out_specs=spec, check_vma=False)
```

time: 1080 us -> 91.7 us (0.08)
  waiting for transfers between devices: 854 us -> 0 us
  other arithmetic: 142 us -> 0.05 us
  Pallas kernels: 0 us -> 87.6 us
  local copies, waits for them, and re-layouts: 37.2 us -> 2.92 us
  matrix products: 20 us -> 0 us
  between operations: 17.5 us -> 0.94 us
    psum x6 -> x0, waiting for transfers between devices: 853 us -> none  [broadcast(): return lax.psum(block, axis)]
    another operation x23 -> x1, other arithmetic: 128 us -> 0.05 us  [local(): jnp.stack([block(0, r // 16), block(top, (r - 1 + 32 * top) // 16), block...]
    pallas_call x0 -> x2, Pallas kernels: none -> 87.6 us  [the longest x1 80 us: local(): pl.pallas_call(gather_kernel, out_shape=(jax.ShapeDtypeStruct((2, 2, B, B...]
    another operation x21 -> x1, local copies, waits for them, and re-layouts: 17 us -> 0.04 us  [local(): jnp.stack([block(0, r // 16), block(top, (r - 1 + 32 * top) // 16), block...]
    another operation x10 -> x0, matrix products: 11.8 us -> none  [the longest x6 6.21 us: solve_blocks(): jax.scipy.linalg.solve_triangular(diag_lower, flattened, lower=True)]
  transfers between devices with their start and end apart: 6 -> 0, of which waited for: 6 -> 0; matrix products, arithmetic and copies ran while one was open for 1% -> 0% of each run, Pallas kernels for 0% -> 0%
where the time goes in v1:
time: 91.7 us; the launch traced here: 91.5 us
  Pallas kernels  87.6 us (96%)
  local copies, waits for them, and re-layouts  2.92 us (3%)
  between operations  0.94 us (1%)
    pallas_call x1, Pallas kernels, local(): pl.pallas_call(gather_kernel, out_shape=(jax.ShapeDtypeStruct((2, 2, B, B...  80 us
    pallas_call x1, Pallas kernels, local(): pl.pallas_call(update_kernel, out_shape=jax.ShapeDtypeStruct(matrix.shape...  7.62 us
    dynamic_slice x1, local copies, waits for them, and re-layouts, local(): x = lax.dynamic_index_in_dim(matrix, t, 2, keepdims=False)  2.13 us

profile of v1, /device:TPU:56, one launch (start us, length us, event | category | flops | bytes accessed | tf_op | source)
XLA Modules:
  0.0 91.5 jit_solution(10705419277455852247)
XLA Ops:
  0.0 0.0 copy-start
  0.9 2.1 %constant_dynamic-slice_fusion.3 = f32[2,256,1,256]{3,2,1,0:T(1,128)S(1)} fusion(f32[2,256,4,256]{3,2,1,0:T(4,128)} %m_ref.1, s32[]{:T(128)S(6)} %select_n.45), kind=kLoop, calls=%fused_computation.8 | loop fusion | bytes 1048580 | tf_op jit(solution)/shard_map/jit(dynamic_index_in_dim)/dynamic_slice | solution.py:427
  3.0 0.0 copy-done
  3.1 0.7 constant_dynamic-slice_fusion.2
  3.8 0.1 pad_maximum_fusion.e_ref
  3.9 0.0 copy-start.1
  3.9 80.0 %gather_factor.1 = (f32[2,2,256,256]{3,2,1,0:T(8,128)S(1)}, f32[2,2,2,256,256]{4,3,2,1,0:T(8,128)S(1)}, f32[3,256,256]{2,1,0:T(8,128)S(1)}) custom-call(s32[1]{0:T(128)} %copy.18.k_ref, f32[2,256,256]{2,1,0:T(8,128)S(1)} %bitcast.16, f32[3,256,256]{2,1,0:T(8,128)S(1)} %pad_maximum_fusion.e_ref), custom_call_target="tpu_custom_call" | custom-call | flops 1000000000 | bytes 10000000 | tf_op jit(solution)/shard_map/gather_factor/pallas_call | solution.py:435
  83.9 0.0 copy-done.1
  83.9 7.6 %update.1 = f32[2,256,4,256]{3,2,1,0:T(4,128)} custom-call(s32[1]{0:T(128)} %copy.18.k_ref, s32[64,64]{1,0:T(8,128)S(1)} %copy-done.1, f32[2,256,4,256]{3,2,1,0:T(4,128)S(1)} %copy-done, f32[2,2,256,256]{3,2,1,0:T(8,128)S(1)} %get-tuple-element.8.rows_ref, f32[2,2,2,256,256]{4,3,2,1,0:T(8,128)S(1)} %get-tuple-element.9.cols_ref, ...), custom_call_target="tpu_custom_call" | custom-call | flops 4000000000 | bytes 10000000 | tf_op jit(solution)/shard_map/update/pallas_call | solution.py:458
  (3 shorter events, 0.1 us)
Async XLA Ops:
  0.0 3.0 %copy-start = (f32[2,256,4,256]{3,2,1,0:T(4,128)S(1)}, f32[2,256,4,256]{3,2,1,0:T(4,128)}, u32[]{:S(2)}) copy-start(f32[2,256,4,256]{3,2,1,0:T(4,128)} %m_ref.1) | copy-start | bytes 6291460
  3.9 80.0 %copy-start.1 = (s32[64,64]{1,0:T(8,128)S(1)}, s32[64,64]{1,0:T(8,128)}, u32[]{:S(2)}) copy-start(s32[64,64]{1,0:T(8,128)} %mask_ref.1) | copy-start | bytes 49156

commit v2 on v1

v2 whole, which is shorter than its diff:
```python
import functools
import jax
import jax.numpy as jnp
from jax import lax
from jax.experimental import pallas as pl
from jax.experimental.pallas import tpu as pltpu
from jax.sharding import PartitionSpec as P

MESH = pl.DeviceIdType.MESH
HI = lax.Precision.HIGHEST
F32 = jnp.float32
B = 256
NB = 16


def piece_row(c):
    return NB * ((c % 2) * 8 + ((c // 2) % 2) * 4 + c // 4)


def tdot(a, b):
    return lax.dot_general(a, b, (((0,), (0,)), ((), ())), precision=HI, preferred_element_type=F32)


def ndot(a, b):
    return lax.dot_general(a, b, (((1,), (1,)), ((), ())), precision=HI, preferred_element_type=F32)


def inverse_factor(m, w, hook):
    rows = lax.broadcasted_iota(jnp.int32, (NB, 128), 0)
    lane = lax.broadcasted_iota(jnp.int32, (NB, B), 1)
    sub = lax.broadcasted_iota(jnp.int32, (NB, B), 0)
    nxt = m[0:NB, :]
    for p in range(B // NB):
        p0, q = p * NB, p * NB + NB
        inside = (lane >= p0) & (lane < q)
        t = [jnp.broadcast_to(nxt[:, p0 + c : p0 + c + 1], (NB, 128)) for c in range(NB)]
        x = jnp.where(inside, jnp.where(lane - p0 == sub, 1.0, 0.0), nxt)
        x0, x1 = x[:, :128], x[:, 128:]
        s = jnp.ones((NB, 128), F32)
        for j in range(NB):
            d = jnp.broadcast_to(t[j][j : j + 1, :], (NB, 128))
            s = jnp.where(rows == j, lax.rsqrt(d), s)
            mm = jnp.where(rows > j, t[j], 0.0) * (1.0 / d)
            for c in range(j + 1, NB):
                t[c] = t[c] - mm * jnp.broadcast_to(t[c][j : j + 1, :], (NB, 128))
            x0 = x0 - mm * jnp.broadcast_to(x0[j : j + 1, :], (NB, 128))
            x1 = x1 - mm * jnp.broadcast_to(x1[j : j + 1, :], (NB, 128))
        rr = jnp.concatenate([x0 * s, x1 * s], axis=1)
        w[p0:q, :] = jnp.where(lane < q, rr, 0.0)
        if q < B:
            nxt = jnp.where(inside, 0.0, m[q : q + NB, :]) - tdot(rr[:, q : q + NB], rr)
        if q + NB < B:
            wide = lax.broadcasted_iota(jnp.int32, (B - q - NB, B), 1)
            rest = m[q + NB :, :]
            m[q + NB :, :] = jnp.where((wide >= p0) & (wide < q), 0.0, rest) - tdot(rr[:, q + NB :], rr)
        hook(p)


def gather_kernel(
    k_in, m_ref, rows_ref, cols_ref, fac_ref, blk,
    k_ref, k_sem, xs, rsb0, rsb1, hb, low, g12, work, ld,
    rs_s, rs_r, g_s, g_r, cs_s, cs_r, ag_s, ag_r, sib_s, sib_r, zc_s, zc_r, xc_s, xc_r, xf_s, xf_r,
    w_s, w_r,
):
    rsb = (rsb0, rsb1)
    r, c = lax.axis_index("prow"), lax.axis_index("pcol")
    z, x, y, h = r // 4, r % 4, c // 2, c % 2
    cand = (r % 16) == c
    u, rest = r // 16, r % 16
    to_col = (c + 16 * u, rest)
    below = (r + 31) % 32
    home = (below, below % 16)
    is_sub = ((r + 31) % 16) == c

    def at(dz=0, dx=0, dy=0, core=None):
        zz, xx, yy = (z + dz) % 8, (x + dx) % 4, (y + dy) % 8
        return (zz * 4 + xx, yy * 2 + (h if core is None else core))

    def relay_y(zz, m):
        return (2 * zz + (5, 3)[m] + zz // 4) % 8

    on_line = (y == relay_y(z, 0), y == relay_y(z, 1))
    first_holder = on_line[0] & (x == 0)

    def remote(src, dst, ss, rs, to):
        return pltpu.make_async_remote_copy(
            src_ref=src, dst_ref=dst, send_sem=ss, recv_sem=rs, device_id=to, device_id_type=MESH
        )

    def drain(ref, sem):
        pltpu.make_async_copy(ref, ref, sem).wait()

    k_copy = pltpu.make_async_copy(k_in, k_ref, k_sem)
    k_copy.start()
    loads = [
        pltpu.make_async_copy(m_ref.at[s, :, t, :], blk.at[s, t], ld.at[s, t])
        for t in range(4) for s in range(2)
    ]
    for cp in loads:
        cp.start()
    top = jnp.where(r == 0, 1, 0)
    sub_block = blk.at[top, (below) // 16]
    next_block = blk.at[top, r // 16 + 2 * top]
    bar = pltpu.get_barrier_semaphore()

    def greet(to):
        pl.semaphore_signal(bar, inc=1, device_id=to, device_id_type=MESH)

    for j in range(1, 16):
        greet((r, (c + j) % 16))
    for j in range(1, 8):
        greet(at(dz=j))
    for j in range(1, 4):
        greet(at(dx=j))

    @pl.when(jnp.logical_not(cand))
    def _():
        greet((c + 16 * u, rest))

    @pl.when(cand)
    def _():
        up = (r + 1) % 32
        greet((up, up % 16))
        greet((up, r % 16))

    @pl.when(first_holder | on_line[1])
    def _():
        def one(i, carry):
            greet((i, i % 16))
            return carry

        lax.fori_loop(0, 32, one, 0)

    arrivals = 15 + 7 + 3 + jnp.where(cand, 81, 1) + jnp.where(is_sub, 1, 0)
    mine = pl.ds(pl.multiple_of(piece_row(c), NB), NB)

    def first_sends():
        pl.semaphore_wait(bar, arrivals)

        @pl.when(is_sub)
        def _():
            remote(sub_block, g12.at[0], g_s.at[0], g_r.at[0], home).start()

        @pl.when(cand)
        def _():
            remote(next_block, g12.at[1], g_s.at[1], g_r.at[1], home).start()

        for s in range(2):
            for j in range(1, 16):
                to = (c + j) % 16
                row = pl.multiple_of(piece_row(to), NB)
                remote(xs.at[s, pl.ds(row, NB), :], rsb[s].at[c], rs_s.at[s], rs_r.at[s], (r, to)).start()

    for cp in loads:
        cp.wait()
    k_copy.wait()
    k = k_ref[0]
    slot = jnp.where(c == k % 16, k // 16, (k + 1) // 16)
    xs[...] = blk[:, slot]
    rsb0[c] = xs[0, mine, :]
    rsb1[c] = xs[1, mine, :]
    theirs = pl.ds(pl.multiple_of(piece_row(rest), NB), NB)

    def pick_rows(s):
        drain(rsb[s].at[pl.ds(0, 15)], rs_r.at[s])
        rows_ref[0, s, mine, :] = rsb[s][k % 16]
        rows_ref[1, s, mine, :] = rsb[s][(k + 1) % 16]

        @pl.when(jnp.logical_not(cand))
        def _():
            piece = rows_ref.at[:, s, mine, :]
            remote(piece, cols_ref.at[u, :, s, mine, :], cs_s.at[s], cs_r.at[s], to_col).start()

        @pl.when(cand)
        def _():
            cols_ref[u, :, s, mine, :] = rows_ref[:, s, mine, :]

    def send_y():
        piece = rows_ref.at[:, :, mine, :]
        for j in range(1, 8):
            remote(piece, piece, ag_s, ag_r, at(dy=j)).start()

    def send_z(s):
        piece = cols_ref.at[u, :, s, theirs, :]

        @pl.when(jnp.logical_not(cand))
        def _():
            drain(piece, cs_r.at[s])

        for j in range(1, 8):
            remote(piece, piece, zc_s.at[s], zc_r.at[s], at(dz=j)).start()

    def send_sibling():
        drain(rows_ref.at[:, :, pl.ds(0, 7 * NB), :], ag_r)
        half = rows_ref.at[:, :, pl.ds(pl.multiple_of(128 * h, 128), 128), :]
        remote(half, half, sib_s, sib_r, at(core=1 - h)).start()

    def quarter(xx):
        return pl.ds(pl.multiple_of(NB * (8 * (xx % 2) + 4 * ((xx // 2) % 2)), 64), 64)

    def send_x(s):
        drain(cols_ref.at[0, :, s, pl.ds(0, 7 * NB), :], zc_r.at[s])
        part = cols_ref.at[:, :, s, quarter(x), :]
        remote(part, part, xc_s.at[s, 0], xc_r.at[s, 0], at(dx=1)).start()
        remote(part, part, xc_s.at[s, 1], xc_r.at[s, 1], at(dx=3)).start()

    def forward_x(s):
        for way, dx in ((0, 1), (1, 3)):
            part = cols_ref.at[:, :, s, quarter(x + 4 - dx), :]
            drain(part, xc_r.at[s, way])
            half = cols_ref.at[way, :, s, quarter(x + 4 - dx), :]
            remote(half, half, xf_s.at[s, way], xf_r.at[s, way], at(dx=dx)).start()

    def scatter_factor(f, pieces=range(16)):
        for p in pieces:
            zz, core = p % 8, p // 8
            src = low.at[f, pl.ds(p * NB, NB), :]
            if f < 2:
                to = (zz * 4, relay_y(zz, 0) * 2 + core)
                remote(src, hb.at[f, r], w_s.at[0, f], w_r.at[0, f], to).start()
            else:
                for xx in range(4):
                    to = (zz * 4 + xx, relay_y(zz, 1) * 2 + core)
                    remote(src, hb.at[0, r], w_s.at[1, 0], w_r.at[1, 0], to).start()

    slab = pl.ds(pl.multiple_of(128 * h + NB * z, NB), NB)
    side = pl.ds(pl.multiple_of(128 * h, 128), 128)

    def relay_first(stage):
        piece = fac_ref.at[pl.ds(0, 2), slab, :]
        if stage == 0:

            @pl.when(first_holder)
            def _():
                drain(hb.at[0], w_r.at[0, 0])
                drain(hb.at[1], w_r.at[0, 1])
                fac_ref[0, slab, :] = hb[0, k]
                fac_ref[1, slab, :] = hb[1, k]
                for j in range(1, 4):
                    remote(piece, piece, w_s.at[0, 2], w_r.at[0, 2], at(dx=j)).start()

        elif stage == 1:

            @pl.when(on_line[0])
            def _():
                @pl.when(x != 0)
                def _():
                    drain(piece, w_r.at[0, 2])

                for j in range(1, 8):
                    remote(piece, piece, w_s.at[0, 3], w_r.at[0, 3], at(dy=j)).start()

        elif stage == 2:

            @pl.when(jnp.logical_not(on_line[0]))
            def _():
                drain(piece, w_r.at[0, 3])

            for j in range(1, 8):
                remote(piece, piece, w_s.at[0, 4], w_r.at[0, 4], at(dz=j)).start()
        else:
            drain(fac_ref.at[pl.ds(0, 2), pl.ds(0, 7 * NB), :], w_r.at[0, 4])
            half = fac_ref.at[pl.ds(0, 2), side, :]
            remote(half, half, w_s.at[0, 5], w_r.at[0, 5], at(core=1 - h)).start()

    def relay_last(stage):
        piece = fac_ref.at[2, slab, :]
        if stage == 0:

            @pl.when(on_line[1])
            def _():
                drain(hb.at[0], w_r.at[1, 0])
                fac_ref[2, slab, :] = hb[0, k]
                for j in range(1, 8):
                    remote(piece, piece, w_s.at[1, 3], w_r.at[1, 3], at(dy=j)).start()

        elif stage == 1:

            @pl.when(jnp.logical_not(on_line[1]))
            def _():
                drain(piece, w_r.at[1, 3])

            for j in range(1, 8):
                remote(piece, piece, w_s.at[1, 4], w_r.at[1, 4], at(dz=j)).start()
        else:
            drain(fac_ref.at[2, pl.ds(0, 7 * NB), :], w_r.at[1, 4])
            half = fac_ref.at[2, side, :]
            remote(half, half, w_s.at[1, 5], w_r.at[1, 5], at(core=1 - h)).start()

    eye = jnp.where(
        lax.broadcasted_iota(jnp.int32, (B, B), 0) == lax.broadcasted_iota(jnp.int32, (B, B), 1), 1.0, 0.0
    ).astype(F32)

    @pl.when(cand)
    def _():
        a = blk[0, r // 16]
        work[...] = (a + a.T) * 0.5 + eye

        def first_hook(p):
            if p == 4:
                first_sends()
                scatter_factor(0, range(5))
            elif p > 4:
                scatter_factor(0, [p])

        inverse_factor(work, low.at[0], first_hook)
        drain(g12.at[0], g_r.at[0])
        drain(g12.at[1], g_r.at[1])
        l21 = ndot(g12[0], low[0])
        low[1] = l21
        scatter_factor(1)
        d = g12[1]
        work[...] = (d + d.T) * 0.5 + eye - ndot(l21, l21)

        pick_rows(0)

        def second_hook(p):
            scatter_factor(2, [p])
            for when, step in plan:
                if when == p:
                    step()

        plan = (
            (1, lambda: pick_rows(1)),
            (2, send_y),
            (3, lambda: send_z(0)),
            (7, lambda: send_z(1)),
            (10, lambda: relay_first(1)),
            (12, lambda: send_x(0)),
            (15, lambda: relay_first(2)),
        )
        inverse_factor(work, low.at[2], second_hook)

    @pl.when(jnp.logical_not(cand))
    def _():
        first_sends()
        pick_rows(0)
        pick_rows(1)
        send_y()
        send_z(0)
        send_z(1)
        relay_first(0)
        relay_first(1)
        send_x(0)
        relay_first(2)

    send_x(1)
    send_sibling()
    forward_x(0)
    relay_first(3)
    relay_last(0)
    relay_last(1)
    forward_x(1)
    relay_last(2)

    drain(fac_ref.at[pl.ds(0, 2), pl.ds(0, 128), :], w_r.at[0, 5])
    drain(fac_ref.at[2, pl.ds(0, 128), :], w_r.at[1, 5])
    drain(rows_ref.at[:, :, pl.ds(0, 128), :], sib_r)
    for s in range(2):
        for way in range(2):
            drain(cols_ref.at[way, :, s, quarter(x + 2), :], xf_r.at[s, way])

    @pl.when(is_sub)
    def _():
        drain(g12.at[0], g_s.at[0])

    @pl.when(cand)
    def _():
        drain(g12.at[0], g_s.at[1])
        drain(low.at[0], w_s.at[0, 0])
        drain(low.at[0], w_s.at[0, 1])
        drain(hb.at[:, pl.ds(0, 32)], w_s.at[1, 0])

    drain(rows_ref.at[:, :, pl.ds(0, 7 * NB), :], ag_s)
    drain(rows_ref.at[:, :, pl.ds(0, 128), :], sib_s)
    for s in range(2):
        drain(rsb[s].at[pl.ds(0, 15)], rs_s.at[s])

        @pl.when(jnp.logical_not(cand))
        def _():
            drain(rows_ref.at[:, s, mine, :], cs_s.at[s])

        drain(cols_ref.at[0, :, s, pl.ds(0, 7 * NB), :], zc_s.at[s])
        for way in range(2):
            drain(cols_ref.at[:, :, s, quarter(x), :], xc_s.at[s, way])
            drain(cols_ref.at[way, :, s, quarter(x), :], xf_s.at[s, way])

    @pl.when(first_holder)
    def _():
        drain(fac_ref.at[pl.ds(0, 2), pl.ds(0, 3 * NB), :], w_s.at[0, 2])

    @pl.when(on_line[0])
    def _():
        drain(fac_ref.at[pl.ds(0, 2), pl.ds(0, 7 * NB), :], w_s.at[0, 3])

    @pl.when(on_line[1])
    def _():
        drain(fac_ref.at[2, pl.ds(0, 7 * NB), :], w_s.at[1, 3])

    drain(fac_ref.at[pl.ds(0, 2), pl.ds(0, 7 * NB), :], w_s.at[0, 4])
    drain(fac_ref.at[2, pl.ds(0, 7 * NB), :], w_s.at[1, 4])
    drain(fac_ref.at[pl.ds(0, 2), pl.ds(0, 128), :], w_s.at[0, 5])
    drain(fac_ref.at[2, pl.ds(0, 128), :], w_s.at[1, 5])


def split(a):
    hi = a.astype(jnp.bfloat16)
    return hi, (a - hi.astype(F32)).astype(jnp.bfloat16)


def dot3(a, b):
    dims = (((1,), (1,)), ((), ()))
    one = lambda u, v: lax.dot_general(u, v, dims, preferred_element_type=F32)
    return one(a[0], b[0]) + (one(a[0], b[1]) + one(a[1], b[0]))


def update_kernel(k_ref, mask_ref, m_ref, rows_ref, cols_ref, fac_ref, out_ref, l1h, l1l, l2h, l2l):
    r, c = lax.axis_index("prow"), lax.axis_index("pcol")
    k = k_ref[0]
    n = k + 1
    w1, l21, w2 = split(fac_ref[0]), split(fac_ref[1]), split(fac_ref[2])

    ids = [r, r + 32, c, c + 32, c + 16, c + 48]
    for v, i in enumerate(ids):
        if v < 2:
            a1, a2 = rows_ref[0, v], rows_ref[1, v]
        else:
            a1, a2 = cols_ref[v // 2 - 1, 0, v % 2], cols_ref[v // 2 - 1, 1, v % 2]
        a1 = jnp.where((mask_ref[i, k] == 1) & (i > k), a1, 0.0)
        a2 = jnp.where((mask_ref[i, n] == 1) & (i > n), a2, 0.0)
        p1 = split(dot3(split(a1), w1))
        a2 = jnp.where(i > n, a2 - dot3(p1, l21), 0.0)
        p2 = split(dot3(split(a2), w2))
        l1h[v], l1l[v] = p1
        l2h[v], l2l[v] = p2

    col_slot = [2, 4, 3, 5]
    for s in range(2):
        i = r + 32 * s
        for t in range(4):
            j = c + 16 * t
            v = col_slot[t]
            lower = i >= j
            if s == 0 and t >= 2:
                out_ref[s, :, t, :] = jnp.zeros((B, B), F32)
                continue
            base = jnp.where((mask_ref[i, j] == 1) & lower, m_ref[s, t], 0.0)
            upd = dot3((l1h[s], l1l[s]), (l1h[v], l1l[v])) + dot3((l2h[s], l2l[s]), (l2h[v], l2l[v]))
            out_ref[s, :, t, :] = base - jnp.where(lower, upd, 0.0)

    eye = jnp.where(
        lax.broadcasted_iota(jnp.int32, (B, B), 0) == lax.broadcasted_iota(jnp.int32, (B, B), 1), 1.0, 0.0
    ).astype(F32)
    for s in range(2):
        i = r + 32 * s
        for t in range(3):
            j = c + 16 * t

            @pl.when((j == k) & (i > k))
            def _():
                out_ref[s, :, t, :] = l1h[s].astype(F32) + l1l[s].astype(F32)

            @pl.when((j == n) & (i > n))
            def _():
                out_ref[s, :, t, :] = l2h[s].astype(F32) + l2l[s].astype(F32)

            @pl.when((j == k) & (i == k))
            def _():
                a = m_ref[s, t]
                f = ndot((a + a.T) * 0.5 + eye, fac_ref[0])
                low = lax.broadcasted_iota(jnp.int32, (B, B), 0) >= lax.broadcasted_iota(jnp.int32, (B, B), 1)
                out_ref[s, :, t, :] = jnp.where(low, f, 0.0)

            @pl.when((j == n) & (i == n))
            def _():
                a = m_ref[s, t]
                g = fac_ref[1]
                f = ndot((a + a.T) * 0.5 + eye - ndot(g, g), fac_ref[2])
                low = lax.broadcasted_iota(jnp.int32, (B, B), 0) >= lax.broadcasted_iota(jnp.int32, (B, B), 1)
                out_ref[s, :, t, :] = jnp.where(low, f, 0.0)


def vmem():
    return pl.BlockSpec(memory_space=pltpu.VMEM)


def smem():
    return pl.BlockSpec(memory_space=pltpu.SMEM)


def update_call(first_panel, block_mask, blocks, rows, cols, fac):
    return pl.pallas_call(
        update_kernel,
        out_shape=jax.ShapeDtypeStruct((2, B, 4, B), F32),
        in_specs=[smem(), smem(), vmem(), vmem(), vmem(), vmem()],
        out_specs=vmem(),
        scratch_shapes=[pltpu.VMEM((6, B, B), jnp.bfloat16)] * 4,
        compiler_params=pltpu.CompilerParams(vmem_limit_bytes=48 << 20),
        cost_estimate=pl.CostEstimate(flops=4 * 10**9, bytes_accessed=10**7, transcendentals=0),
        name="update",
    )(first_panel, block_mask, blocks, rows, cols, fac)


def local(matrix, block_mask, first_panel):
    dma = pltpu.SemaphoreType.DMA
    rows, cols, fac, blk = pl.pallas_call(
        gather_kernel,
        out_shape=(
            jax.ShapeDtypeStruct((2, 2, B, B), F32),
            jax.ShapeDtypeStruct((2, 2, 2, B, B), F32),
            jax.ShapeDtypeStruct((3, B, B), F32),
            jax.ShapeDtypeStruct((2, 4, B, B), F32),
        ),
        in_specs=[pl.BlockSpec(memory_space=pl.ANY)] * 2,
        out_specs=(vmem(), vmem(), vmem(), vmem()),
        scratch_shapes=[
            pltpu.SMEM((1,), jnp.int32),
            dma,
            pltpu.VMEM((2, B, B), F32),
            pltpu.VMEM((16, NB, B), F32),
            pltpu.VMEM((16, NB, B), F32),
            pltpu.VMEM((2, 32, NB, B), F32),
            pltpu.VMEM((3, B, B), F32),
            pltpu.VMEM((2, B, B), F32),
            pltpu.VMEM((B, B), F32),
            dma((2, 4)),
            dma((2,)), dma((2,)), dma((2,)), dma((2,)), dma((2,)), dma((2,)), dma, dma, dma, dma, dma((2,)), dma((2,)),
            dma((2, 2)), dma((2, 2)), dma((2, 2)), dma((2, 2)), dma((2, 6)), dma((2, 6)),
        ],
        compiler_params=pltpu.CompilerParams(collective_id=0, has_side_effects=True, vmem_limit_bytes=40 << 20),
        cost_estimate=pl.CostEstimate(flops=10**9, bytes_accessed=10**7, transcendentals=0),
        name="gather_factor",
    )(first_panel, matrix)
    return update_call(first_panel, block_mask, blk, rows, cols, fac)


def solution(mesh):
    spec = P(None, "prow", None, "pcol")
    return jax.shard_map(local, mesh=mesh, in_specs=(spec, P(), P()), out_specs=spec, check_vma=False)
```

time: 91.7 us -> 82.5 us (0.90)
  the two profiles are of different devices: /device:TPU:56 before, /device:TPU:5 now
where the time goes in v2:
time: 82.5 us; the launch traced here: 82.3 us
  Pallas kernels  80.1 us (97%)
  local copies, waits for them, and re-layouts  1.59 us (2%)
    pallas_call x1, Pallas kernels, local(): pl.pallas_call(gather_kernel, out_shape=(jax.ShapeDtypeStruct((2, 2, B, B...  72.9 us
    pallas_call x1, Pallas kernels, update_call(): pl.pallas_call(update_kernel, out_shape=jax.ShapeDtypeStruct((2, B, 4, B)...  7.17 us

profile of v2, /device:TPU:5, one launch (start us, length us, event | category | flops | bytes accessed | tf_op | source)
XLA Modules:
  0.0 82.3 jit_solution(13043973237203780233)
XLA Ops:
  0.7 0.0 copy-start
  0.7 1.6 %copy-done = f32[2,256,4,256]{3,2,1,0:T(4,128)S(1)} copy-done((f32[2,256,4,256]{3,2,1,0:T(4,128)S(1)}, f32[2,256,4,256]{3,2,1,0:T(4,128)}, u32[]{:S(2)}) %copy-start) | copy-done | bytes 2097176
  2.2 0.0 copy-start.1
  2.2 72.9 %gather_factor.1 = (f32[2,2,256,256]{3,2,1,0:T(8,128)S(1)}, f32[2,2,2,256,256]{4,3,2,1,0:T(8,128)S(1)}, f32[3,256,256]{2,1,0:T(8,128)S(1)}, f32[2,4,256,256]{3,2,1,0:T(8,128)S(1)}) custom-call(s32[1]{0:T(128)S(6)} %copy.4.k_in.k_ref, f32[2,256,4,256]{3,2,1,0:T(4,128)S(1)} %copy-done), custom_call_target="tpu_custom_call" | custom-call | flops 1000000000 | bytes 10000000 | tf_op jit(solution)/shard_map/gather_factor/pallas_call | solution.py:506
  75.2 0.0 copy-done.1
  75.2 7.2 %update.1 = f32[2,256,4,256]{3,2,1,0:T(4,128)} custom-call(s32[1]{0:T(128)S(6)} %copy.4.k_in.k_ref, s32[64,64]{1,0:T(8,128)S(1)} %copy-done.1, f32[2,4,256,256]{3,2,1,0:T(8,128)S(1)} %get-tuple-element.9.m_ref, f32[2,2,256,256]{3,2,1,0:T(8,128)S(1)} %get-tuple-element.10.rows_ref, f32[2,2,2,256,256]{4,3,2,1,0:T(8,128)S(1)} %get-tuple-element.11.cols_ref, ...), custom_call_target="tpu_custom_call" | custom-call | flops 4000000000 | bytes 10000000 | tf_op jit(solution)/shard_map/update/pallas_call | solution.py:492
Async XLA Ops:
  0.7 1.6 %copy-start = (f32[2,256,4,256]{3,2,1,0:T(4,128)S(1)}, f32[2,256,4,256]{3,2,1,0:T(4,128)}, u32[]{:S(2)}) copy-start(f32[2,256,4,256]{3,2,1,0:T(4,128)} %m_ref.1) | copy-start | bytes 6291460
  2.2 72.9 %copy-start.1 = (s32[64,64]{1,0:T(8,128)S(1)}, s32[64,64]{1,0:T(8,128)}, u32[]{:S(2)}) copy-start(s32[64,64]{1,0:T(8,128)} %mask_ref.1) | copy-start | bytes 49156

commit v3 on v2

--- a/solution.py
+++ b/solution.py
@@ -302,6 +302,8 @@
                 scatter_factor(0, range(5))
             elif p > 4:
                 scatter_factor(0, [p])
+            if p == 15:
+                pick_rows(0)
 
         inverse_factor(work, low.at[0], first_hook)
         drain(g12.at[0], g_r.at[0])
@@ -312,7 +314,6 @@
         d = g12[1]
         work[...] = (d + d.T) * 0.5 + eye - ndot(l21, l21)
 
-        pick_rows(0)
 
         def second_hook(p):
             scatter_factor(2, [p])
@@ -321,36 +322,37 @@
                     step()
 
         plan = (
-            (1, lambda: pick_rows(1)),
-            (2, send_y),
-            (3, lambda: send_z(0)),
-            (7, lambda: send_z(1)),
-            (10, lambda: relay_first(1)),
-            (12, lambda: send_x(0)),
-            (15, lambda: relay_first(2)),
+            (0, lambda: send_z(0)),
+            (2, lambda: pick_rows(1)),
+            (4, lambda: send_z(1)),
+            (5, send_y),
+            (11, lambda: send_x(0)),
+            (13, lambda: relay_first(1)),
         )
         inverse_factor(work, low.at[2], second_hook)
+        send_x(1)
+        relay_first(2)
 
     @pl.when(jnp.logical_not(cand))
     def _():
         first_sends()
         pick_rows(0)
+        send_z(0)
         pick_rows(1)
+        send_z(1)
         send_y()
-        send_z(0)
-        send_z(1)
         relay_first(0)
         relay_first(1)
         send_x(0)
+        send_x(1)
         relay_first(2)
-
-    send_x(1)
+        relay_last(0)
+
+    forward_x(0)
     send_sibling()
-    forward_x(0)
-    relay_first(3)
-    relay_last(0)
     relay_last(1)
     forward_x(1)
+    relay_first(3)
     relay_last(2)
 
     drain(fac_ref.at[pl.ds(0, 2), pl.ds(0, 128), :], w_r.at[0, 5])

time: 82.5 us -> 80.3 us (0.973)
  the two profiles are of different devices: /device:TPU:5 before, /device:TPU:17 now
where the time goes in v3:
time: 80.3 us; the launch traced here: 80.1 us
  Pallas kernels  77.8 us (97%)
  local copies, waits for them, and re-layouts  1.59 us (2%)
    pallas_call x1, Pallas kernels, local(): pl.pallas_call(gather_kernel, out_shape=(jax.ShapeDtypeStruct((2, 2, B, B...  70.7 us
    pallas_call x1, Pallas kernels, update_call(): pl.pallas_call(update_kernel, out_shape=jax.ShapeDtypeStruct((2, B, 4, B)...  7.17 us

profile of v3, /device:TPU:17, one launch (start us, length us, event | category | flops | bytes accessed | tf_op | source)
XLA Modules:
  0.0 80.1 jit_solution(4003111171145476792)
XLA Ops:
  0.7 0.0 copy-start
  0.7 1.6 %copy-done = f32[2,256,4,256]{3,2,1,0:T(4,128)S(1)} copy-done((f32[2,256,4,256]{3,2,1,0:T(4,128)S(1)}, f32[2,256,4,256]{3,2,1,0:T(4,128)}, u32[]{:S(2)}) %copy-start) | copy-done | bytes 2097176
  2.2 0.0 copy-start.1
  2.2 70.7 %gather_factor.1 = (f32[2,2,256,256]{3,2,1,0:T(8,128)S(1)}, f32[2,2,2,256,256]{4,3,2,1,0:T(8,128)S(1)}, f32[3,256,256]{2,1,0:T(8,128)S(1)}, f32[2,4,256,256]{3,2,1,0:T(8,128)S(1)}) custom-call(s32[1]{0:T(128)S(6)} %copy.4.k_in.k_ref, f32[2,256,4,256]{3,2,1,0:T(4,128)S(1)} %copy-done), custom_call_target="tpu_custom_call" | custom-call | flops 1000000000 | bytes 10000000 | tf_op jit(solution)/shard_map/gather_factor/pallas_call | solution.py:508
  72.9 0.0 copy-done.1
  72.9 7.2 %update.1 = f32[2,256,4,256]{3,2,1,0:T(4,128)} custom-call(s32[1]{0:T(128)S(6)} %copy.4.k_in.k_ref, s32[64,64]{1,0:T(8,128)S(1)} %copy-done.1, f32[2,4,256,256]{3,2,1,0:T(8,128)S(1)} %get-tuple-element.9.m_ref, f32[2,2,256,256]{3,2,1,0:T(8,128)S(1)} %get-tuple-element.10.rows_ref, f32[2,2,2,256,256]{4,3,2,1,0:T(8,128)S(1)} %get-tuple-element.11.cols_ref, ...), custom_call_target="tpu_custom_call" | custom-call | flops 4000000000 | bytes 10000000 | tf_op jit(solution)/shard_map/update/pallas_call | solution.py:494
Async XLA Ops:
  0.7 1.6 %copy-start = (f32[2,256,4,256]{3,2,1,0:T(4,128)S(1)}, f32[2,256,4,256]{3,2,1,0:T(4,128)}, u32[]{:S(2)}) copy-start(f32[2,256,4,256]{3,2,1,0:T(4,128)} %m_ref.1) | copy-start | bytes 6291460
  2.2 70.7 %copy-start.1 = (s32[64,64]{1,0:T(8,128)S(1)}, s32[64,64]{1,0:T(8,128)}, u32[]{:S(2)}) copy-start(s32[64,64]{1,0:T(8,128)} %mask_ref.1) | copy-start | bytes 49156
